TPU v7x, 32 devices: a whole 2x2x4 slice. The times are simulated.
32 devices in a mesh: group: 2 (over y), tile: 4 (over z), tm: 2 (over x), pol: 2 (over core).
Axes of the slice: x: 2, y: 2, z: 4, core: 2. Of those that a mesh axis runs over, the one named last changes fastest.
Arguments:
- measured_correlations: float32 [16, 2, 8, 2, 128], P(('group', 'tile', 'tm'), 'pol'), parts along dimension 0, may hold values from -6 to 6
- subpixel_coordinates: float32 [16, 8, 2, 128], P(('group', 'tile', 'tm')), parts along dimension 0, may hold values from 0 to 1
- kernel_start_pixel: int32 [16, 8, 128], P(('group', 'tile', 'tm')), parts along dimension 0, may hold values from 0 to 250360, as said below
- antenna_pairs_per_group: int32 [16, 8, 2], P(('group', 'tile', 'tm')), parts along dimension 0, may hold values from 0 to 196, as said below
- group_epoch_number_list: int32 [16, 8], P(('group', 'tile', 'tm')), parts along dimension 0, may hold values from 0 to 1
- occupied_group_tallies: int32 [16, 4], P(('group', 'tile', 'tm')), parts along dimension 0, may hold values from 0 to 2, as said below
- predicted_fourier_plane: bfloat16 [2, 8, 2, 496, 512], P('pol', ('group', 'tile')), parts along dimension 1, may hold values from -6 to 6
- pointing_errors: float32 [2, 4, 256], P(None, 'group'), parts along dimension 1, may hold values from -2.5 to 2.5
Outputs:
- residual: float32 [16, 2, 8, 2, 128], P(('group', 'tile', 'tm'), 'pol'), parts along dimension 0
- gradient: float32 [2, 1024], P(None, ('group', 'tile', 'tm', 'pol')), parts along dimension 1
There are 2 independent parts, one for each index of `group`. A program takes and returns all parts, laid end to end along the dimension named above; each array names one. Nothing has to cross between parts.
Inputs may be any that keep to these rules, and one draw needn't show every extreme that they name: `kernel_start_pixel`: iu * 512 + iv with iu <= 488 and iv <= 504, so the patch lies inside its tile. `antenna_pairs_per_group`: two different antennas of the 197 dishes. Holder h lies on tile-axis index t = h * 4 // 8; occupied_group_tallies[h, (t + 1) mod 4] is 2, occupied_group_tallies[h, (t + 2) mod 4] is 1, and every other tile of h has at most 1 filled slots.
All inputs are finite; a program needn't handle non-finite values.
Results may differ from a plain program's by a relative error of at most 0.0003.
Values sent between devices are 32-bit elements; how exact they have to be, the bound alone decides.
A program may use at most 256 MiB of HBM per device.

v0:
```python
import math

import jax
import jax.numpy as jnp
from jax import lax
from jax.sharding import PartitionSpec as P

SUPPORT = 8
DISH_COUNT = 197


SHIFT_GAIN = 0.5
BELL_WIDTH = 1.5


def kernel_taper(fraction, shift_cells, tap_location):
    separation = tap_location[:, None, None] - fraction[None] - shift_cells[None, :, None]
    bell = jnp.exp(-separation * separation / (2.0 * BELL_WIDTH * BELL_WIDTH))
    return (bell, SHIFT_GAIN * separation / (BELL_WIDTH * BELL_WIDTH) * bell)


def pairing_table(group_whole_numbers, dish_columns, key_number):
    columns = jnp.arange(key_number, dtype=jnp.int32)
    leading_key = group_whole_numbers[:, 2] * dish_columns + group_whole_numbers[:, 0]
    trailing_key = group_whole_numbers[:, 2] * dish_columns + group_whole_numbers[:, 1]
    first_hit = (leading_key[:, None] == columns[None, :]).astype(jnp.float32)
    second_hit = (trailing_key[:, None] == columns[None, :]).astype(jnp.float32)
    return first_hit + second_hit


def dish_total(block_totals, group_whole_numbers, dish_columns, key_number):
    selector = pairing_table(group_whole_numbers, dish_columns, key_number)
    return jnp.dot(
        block_totals.T,
        selector,
        precision=lax.Precision.HIGHEST,
        preferred_element_type=jnp.float32,
    )


def owner_terms(
    float_values,
    grid_cell_count,
    group_whole_numbers,
    flattened_grid,
    flattened_offsets,
    patch_column,
    tap_location,
    dish_columns,
):
    key_number = flattened_offsets.shape[1]
    selector = pairing_table(group_whole_numbers, dish_columns, key_number)
    shift_cells = SHIFT_GAIN * jnp.dot(
        flattened_offsets,
        selector.T,
        precision=lax.Precision.HIGHEST,
        preferred_element_type=jnp.float32,
    )
    along_u, slope_u = kernel_taper(float_values[:, 2], shift_cells[0], tap_location)
    along_v, slope_v = kernel_taper(float_values[:, 3], shift_cells[1], tap_location)
    tap_count = along_u.shape[0]
    shape_out = (tap_count * tap_count, float_values.shape[0], float_values.shape[2])
    weights = (along_u[:, None] * along_v[None, :]).reshape(shape_out)
    weights_u = (slope_u[:, None] * along_v[None, :]).reshape(shape_out)
    weights_v = (along_u[:, None] * slope_v[None, :]).reshape(shape_out)
    patch_index = patch_column[:, None, None] + grid_cell_count[None]
    samples = flattened_grid[:, patch_index].astype(jnp.float32)
    model_vis = jnp.sum(weights[None] * samples, axis=1)
    deriv_u = jnp.sum(weights_u[None] * samples, axis=1)
    deriv_v = jnp.sum(weights_v[None] * samples, axis=1)
    residual = jnp.stack([float_values[:, 0], float_values[:, 1]]) - model_vis
    term_u = -2.0 * jnp.sum(residual * deriv_u, axis=0)
    term_v = -2.0 * jnp.sum(residual * deriv_v, axis=0)
    return (jnp.transpose(residual, (1, 0, 2)), jnp.stack([term_u, term_v], axis=1))


def local(
    measured_correlations,
    subpixel_coordinates,
    kernel_start_pixel,
    antenna_pairs_per_group,
    group_epoch_number_list,
    occupied_group_tallies,
    predicted_fourier_plane,
    pointing_errors,
):
    float_values = jnp.concatenate([measured_correlations[0, 0], subpixel_coordinates[0]], axis=1)
    grid_cell_count = kernel_start_pixel[0]
    block_list = float_values.shape[0]
    visibility_width = float_values.shape[2]
    tile_total = lax.axis_size("tile")
    capacity = block_list // tile_total
    time_slot_count = pointing_errors.shape[1]
    dish_columns = pointing_errors.shape[2]
    key_number = time_slot_count * dish_columns
    flattened_offsets = pointing_errors.reshape(2, key_number)
    block_order = jnp.arange(block_list, dtype=jnp.int32)
    tile_ids = jnp.arange(tile_total, dtype=jnp.int32)
    tile_counts = jnp.sum(
        jnp.where(
            (block_order // capacity)[:, None] == tile_ids[None, :],
            occupied_group_tallies[0][None, :],
            0,
        ),
        axis=1,
    )
    filled = block_order % capacity < tile_counts
    sent_epoch_entry = jnp.where(filled, group_epoch_number_list[0], time_slot_count)
    group_whole_numbers = jnp.stack(
        [antenna_pairs_per_group[0][:, 0], antenna_pairs_per_group[0][:, 1], sent_epoch_entry],
        axis=1,
    )
    got_floats, got_cells, got_ints = (
        lax.all_to_all(float_values, "tile", split_axis=0, concat_axis=0, tiled=True),
        lax.all_to_all(grid_cell_count, "tile", split_axis=0, concat_axis=0, tiled=True),
        lax.all_to_all(group_whole_numbers, "tile", split_axis=0, concat_axis=0, tiled=True),
    )
    grid_tile = predicted_fourier_plane[0, 0]
    width_v = grid_tile.shape[2]
    flattened_grid = grid_tile.reshape(2, -1)
    tap_ids = jnp.arange(SUPPORT, dtype=jnp.int32)
    patch_column = (tap_ids[:, None] * width_v + tap_ids[None, :]).reshape(-1)
    tap_location = tap_ids.astype(jnp.float32) - (SUPPORT - 1) / 2.0
    received = got_floats.shape[0]
    group_size = math.gcd(received, 32)
    steps_count = received // group_size

    def process(group_item):
        return owner_terms(
            group_item[0],
            group_item[1],
            group_item[2],
            flattened_grid,
            flattened_offsets,
            patch_column,
            tap_location,
            dish_columns,
        )

    grouped = (
        got_floats.reshape((steps_count, group_size) + got_floats.shape[1:]),
        got_cells.reshape((steps_count, group_size) + got_cells.shape[1:]),
        got_ints.reshape((steps_count, group_size) + got_ints.shape[1:]),
    )
    residual_parts, term_parts = lax.map(process, grouped)
    residual = residual_parts.reshape((received,) + residual_parts.shape[2:])
    visit_terms = term_parts.reshape((received,) + term_parts.shape[2:])
    payload = jnp.concatenate([residual, visit_terms], axis=1)
    returned_value = lax.all_to_all(payload, "tile", split_axis=0, concat_axis=0, tiled=True)
    partial_result = dish_total(
        jnp.sum(returned_value[:, 2:4], axis=2), group_whole_numbers, dish_columns, key_number
    )
    home_residual = jnp.where(filled[:, None, None], returned_value[:, 0:2], 0.0)
    holder_list = tile_total * lax.axis_size("tm")
    scale_factor = 1.0 / math.sqrt(
        2.0 * lax.axis_size("pol") * holder_list * block_list * visibility_width / DISH_COUNT
    )
    summed = lax.psum_scatter(
        partial_result, ("tile", "tm", "pol"), scatter_dimension=1, tiled=True
    )
    return (home_residual[None, None], summed * scale_factor)


def solution(mesh):
    return jax.shard_map(
        local,
        mesh=mesh,
        in_specs=(
            P(("group", "tile", "tm"), "pol", None, None, None),
            P(("group", "tile", "tm"), None, None, None),
            P(("group", "tile", "tm"), None, None),
            P(("group", "tile", "tm"), None, None),
            P(("group", "tile", "tm"), None),
            P(("group", "tile", "tm"), None),
            P("pol", ("group", "tile"), None, None, None),
            P(None, "group", None),
        ),
        out_specs=(
            P(("group", "tile", "tm"), "pol", None, None, None),
            P(None, ("group", "tile", "tm", "pol")),
        ),
        check_vma=False,
    )
```

profile of v0, /device:TPU:0, one launch (start us, length us, event | category | flops | bytes accessed | tf_op | source)
XLA Modules:
  0.0 1154.7 jit_solution(377408405672862903)
XLA Ops:
  7.2 0.0 copy-start.4
  7.2 0.0 copy-start.2
  7.2 0.0 copy-start.3
  7.2 0.0 copy-start
  7.2 0.5 broadcast.394
  7.7 1.3 reduce.17
  9.1 0.1 squeeze.51
  9.1 0.7 select_reduce_fusion
  9.9 0.1 reduce_sum.73
  10.0 0.8 stack.18
  10.8 0.7 copy.78
  11.5 6.3 all-to-all-start.1
  17.8 42.0 %copy.79 = bf16[1,1,2,496,512]{2,4,3,1,0:T(8,128)(2,1)} copy(bf16[1,1,2,496,512]{4,3,2,1,0:T(8,128)(2,1)} %param.14) | data formatting | bytes 2031616 | tf_op args[6]
  59.8 0.1 iota_add_fusion
  59.8 0.1 add.144
  59.9 0.1 copy.92
  60.0 0.1 copy.85
  60.1 0.1 copy.84
  60.2 0.6 pad_maximum_fusion.1
  60.8 0.1 copy.93
  60.9 0.0 all-to-all-done.1
  60.9 5.1 all-to-all-start.2
  66.0 0.2 add_reduce_fusion.3
  66.2 0.2 fusion.3
  66.4 5.1 all-to-all-done.2
  71.5 3.2 all-to-all-start
  74.8 0.1 fusion.7
  74.9 972.3 %gather_fusion = bf16[65536,2]{1,0:T(8,128)(2,1)} fusion(bf16[2,253952]{0,1:T(8,128)(2,1)} %bitcast.66, s32[65536]{0:T(1024)S(1)} %fusion.7), kind=kCustom, calls=%fused_computation | custom fusion | bytes 786432 | tf_op jit(solution)/shard_map/while/body/eval_jaxpr/gather | solution.py:67
  1047.2 0.0 all-to-all-done
  1047.2 0.2 copy.80
  1047.4 0.1 multiply_multiply_fusion
  1047.6 0.1 broadcast_multiply_fusion
  1047.6 30.1 %fusion.2 = (f32[8,128,2]{2,1,0:T(8,128)S(1)}, f32[8,128,2]{2,1,0:T(8,128)S(1)}, f32[8,128,2]{2,1,0:T(8,128)S(1)}) fusion(bf16[64,8,128,2]{3,2,1,0:T(8,128)(2,1)} %bitcast.67, f32[64,8,128]{2,1,0:T(8,128)S(1)} %bitcast.70, f32[64,8,128]{2,1,0:T(8,128)S(1)} %bitcast.69, f32[64,8,128]{2,1,0:T(8,128)S(1)} %bitcast.68), kind=kLoop, calls=%fused_computation.6 | loop fusion | flops 911360 | bytes 1073152 | tf_op jit(solution)/shard_map/while/body/eval_jaxpr/reduce_sum | solution.py:69
  1077.7 0.4 fusion.5
  1078.1 0.2 copy.82
  1078.3 0.2 copy.81
  1078.6 0.3 pad_maximum_fusion
  1078.9 0.8 copy.83
  1079.7 5.9 all-to-all-start.3
  1085.6 0.0 reduce-scatter.4.cloned.1.call-start
  1085.6 0.1 add_reduce_fusion.1
  1085.8 5.5 all-to-all-done.3
  1091.3 0.7 slice_reduce_fusion
  1091.9 1.4 convolution_bitcast_fusion
  1093.3 0.0 reduce-scatter.4.cloned.1.call-update
  1093.3 53.1 %reduce-scatter.4.cloned.1.call-done = f32[32,2]{1,0:T(8,128)} async-done(((f32[512,2]{1,0:T(8,128)}), f32[32,2]{1,0:T(8,128)}) %reduce-scatter.4.cloned.1.call-update) | async-done | bytes 272
  1146.5 0.8 copy.89
  1147.2 0.6 broadcast_multiply_fusion.3
  (18 shorter events, 0.1 us)
Async XLA Ops:
  7.2 52.9 %copy-start.4 = (s32[1,8]{1,0:T(1,128)S(1)}, s32[1,8]{1,0:T(1,128)}, u32[]{:S(2)}) copy-start(s32[1,8]{1,0:T(1,128)} %param.12) | copy-start | bytes 100
  7.2 52.7 %copy-start.2 = (s32[1,8,2]{1,2,0:T(2,128)S(1)}, s32[1,8,2]{1,2,0:T(2,128)}, u32[]{:S(2)}) copy-start(s32[1,8,2]{1,2,0:T(2,128)} %param.11) | copy-start | bytes 196
  7.2 52.7 %copy-start.3 = (f32[2,2,256]{2,1,0:T(2,128)S(1)}, f32[2,2,256]{2,1,0:T(2,128)}, u32[]{:S(2)}) copy-start(f32[2,2,256]{2,1,0:T(2,128)} %param.15) | copy-start | bytes 12292
  7.2 53.0 %copy-start = (f32[1,8,2,128]{3,2,1,0:T(2,128)S(1)}, f32[1,8,2,128]{3,2,1,0:T(2,128)}, u32[]{:S(2)}) copy-start(f32[1,8,2,128]{3,2,1,0:T(2,128)} %param.9) | copy-start | bytes 24580
  7.2 53.0 %copy-start.1 = (f32[1,1,8,2,128]{4,3,2,1,0:T(2,128)S(1)}, f32[1,1,8,2,128]{4,3,2,1,0:T(2,128)}, u32[]{:S(2)}) copy-start(f32[1,1,8,2,128]{4,3,2,1,0:T(2,128)} %param.8) | copy-start | bytes 24580
  11.5 49.4 %all-to-all-start.1 = ((s32[4,2,3]{2,1,0:T(2,128)}), s32[4,2,3]{2,1,0:T(2,128)S(1)}, u32[]{:S(2)}, u32[]{:S(2)}) async-start(s32[4,2,3]{2,1,0:T(2,128)} %copy.78), calls=%async_computation.1 | async-start | bytes 8192 | tf_op jit(solution)/shard_map/all_to_all | solution.py:116
  60.9 10.7 all-to-all-start.2
  71.5 975.6 %all-to-all-start = ((f32[8,4,128]{2,1,0:T(4,128)}), f32[8,4,128]{2,1,0:T(4,128)S(1)}, u32[]{:S(2)}, u32[]{:S(2)}) async-start(f32[8,4,128]{2,1,0:T(4,128)} %pad_maximum_fusion.1), calls=%async_computation | async-start | bytes 32768 | tf_op jit(solution)/shard_map/all_to_all | solution.py:114
  1079.7 11.5 all-to-all-start.3
  1085.6 60.8 %reduce-scatter.4.cloned.1.call-start = ((), (), s32[]{:S(2)}) async-start(), calls=%async_computation.5 | async-start | bytes 278528
Sparse Core Ops, SparseCore 0:
  1093.5 52.9 reduce-scatter.3
where the time goes:
time: 1160 us; the launch traced here: 1150 us
  local copies, waits for them, and re-layouts  1020 us (88%)
  waiting for transfers between devices  63.7 us (5%)
  other arithmetic  35.5 us (3%)
  starting transfers between devices  20.6 us (2%)
  between operations  14.2 us (1%)
    gather x1, local copies, waits for them, and re-layouts, owner_terms(): samples = flattened_grid[:, patch_index].astype(jnp.float32)  972 us
    unnamed x2, waiting for transfers between devices  53.1 us
    unnamed x16, local copies, waits for them, and re-layouts  43.4 us
    reduce_sum x1, other arithmetic, owner_terms(): deriv_u = jnp.sum(weights_u[None] * samples, axis=1)  30.1 us
  transfers between devices with their start and end apart: 5, of which 3 were waited for; matrix products, arithmetic and copies ran while one was open for 88% of the time, Pallas kernels for 0%

commit v1 on v0

v1 whole, which is shorter than its diff:
```python
import functools
import math

import jax
import jax.numpy as jnp
from jax import lax
from jax.experimental import pallas as pl
from jax.experimental.pallas import tpu as pltpu
from jax.sharding import PartitionSpec as P

SUPPORT = 8
DISH_COUNT = 197
SHIFT_GAIN = 0.5
BELL_WIDTH = 1.5
AXES = ("group", "tile", "tm", "pol")
MESH = pl.DeviceIdType.MESH


def taps(centre, start):
    row = lax.broadcasted_iota(jnp.int32, (8, start.shape[1]), 0)
    tap = (row - start) & 7
    separation = tap.astype(jnp.float32) - (SUPPORT - 1) / 2.0 - centre
    bell = jnp.exp(-separation * separation / (2.0 * BELL_WIDTH * BELL_WIDTH))
    slope = SHIFT_GAIN * separation / (BELL_WIDTH * BELL_WIDTH) * bell
    return bell, slope, (start + tap) >> 3


def spread(values, hit):
    high = values.astype(jnp.bfloat16).astype(jnp.float32)
    parts = []
    for part in (high, values - high):
        laid = jnp.where(hit, part[None], 0.0)
        parts.append(laid.reshape(-1, laid.shape[2]).astype(jnp.bfloat16))
    return jnp.concatenate(parts, axis=0)


def kernel(
    sizes,
    scale,
    meas_ref,
    sub_ref,
    cell_ref,
    pair_ref,
    epoch_ref,
    tally_ref,
    grid_ref,
    point_ref,
    res_ref,
    grad_ref,
    stage,
    recv,
    out_blocks,
    back,
    part,
    gathered,
    tile_grid,
    grid_sem,
    fwd_send,
    fwd_recv,
    back_send,
    back_recv,
    grad_send,
    grad_recv,
):
    n_tile, n_tm, n_pol = sizes
    count = n_tile * n_tm * n_pol
    group = lax.axis_index("group")
    tile = lax.axis_index("tile")
    tm = lax.axis_index("tm")
    pol = lax.axis_index("pol")
    rows_u, rows_v = grid_ref.shape[3], grid_ref.shape[4]
    width = meas_ref.shape[4]
    columns = point_ref.shape[2]
    own_columns = grad_ref.shape[1]
    slots = n_tile + 1

    load = pltpu.make_async_copy(grid_ref.at[0, 0], tile_grid, grid_sem)
    load.start()

    def peer(k):
        return (
            group,
            lax.rem(tile + k // (n_tm * n_pol), n_tile),
            lax.rem(tm + (k // n_pol) % n_tm, n_tm),
            lax.rem(pol + k % n_pol, n_pol),
        )

    barrier = pltpu.get_barrier_semaphore()

    def greet(k, carry):
        pl.semaphore_signal(barrier, inc=1, device_id=peer(k), device_id_type=MESH)
        return carry

    lax.fori_loop(1, count, greet, 0)

    def block_of(slot):
        if isinstance(slot, int):
            step, half = (slot if slot < 2 else slot - 1), int(slot == 2)
        else:
            step, half = slot - 1, 0
        target = lax.rem(tile + step, n_tile)
        return target, half, 2 * target + half

    def pack(slot):
        target, half, q = block_of(slot)
        time = epoch_ref[0, q]
        first, second = pair_ref[0, q, 0], pair_ref[0, q, 1]
        filled = half < tally_ref[0, target]
        stage[slot, 0:2, :] = meas_ref[0, 0, q]
        sub = sub_ref[0, q]
        for c in range(2):
            shift = SHIFT_GAIN * (point_ref[c, time, first] + point_ref[c, time, second])
            stage[slot, 2 + c : 3 + c, :] = sub[c : c + 1] + shift
        stage[slot, 4:5, :] = cell_ref[0, pl.ds(q, 1), :].astype(jnp.float32)
        for j, antenna in enumerate((first, second)):
            key = jnp.where(filled, time * columns + antenna, -1)
            stage[slot, 5 + j : 6 + j, :] = jnp.full((1, width), key, jnp.int32).astype(jnp.float32)

    def over_slots(body, first):
        for slot in range(first, min(slots, 5)):
            body(slot)
        if slots > 5:
            lax.fori_loop(5, slots, lambda s, c: (body(s), c)[1], 0)

    over_slots(pack, 0)
    part[...] = jnp.zeros_like(part)
    pl.semaphore_wait(barrier, count - 1)

    def first_slot(step):
        return 1 if isinstance(step, int) and step == 1 else step + 1

    def size_of(step):
        return 2 if isinstance(step, int) and step == 1 else 1

    def forward(step):
        span = pl.ds(first_slot(step), size_of(step))
        return pltpu.make_async_remote_copy(
            src_ref=stage.at[span],
            dst_ref=recv.at[span],
            send_sem=fwd_send.at[step],
            recv_sem=fwd_recv.at[step],
            device_id=(group, lax.rem(tile + step, n_tile), tm, pol),
            device_id_type=MESH,
        )

    def backward(step):
        span = pl.ds(first_slot(step), size_of(step))
        return pltpu.make_async_remote_copy(
            src_ref=out_blocks.at[span],
            dst_ref=back.at[span],
            send_sem=back_send.at[step],
            recv_sem=back_recv.at[step],
            device_id=(group, lax.rem(tile - step + n_tile, n_tile), tm, pol),
            device_id_type=MESH,
        )

    def over_steps(body, order=(1, 3, 2)):
        for step in order:
            body(step)
        if n_tile > 4:
            lax.fori_loop(4, n_tile, lambda s, c: (body(s), c)[1], 0)

    over_steps(lambda step: forward(step).start())
    load.wait()

    lane = lax.broadcasted_iota(jnp.int32, part.shape, 2)
    key_here = lax.broadcasted_iota(jnp.int32, part.shape, 0) * own_columns + lane % own_columns
    first_half = lane < own_columns
    inside = lane < 2 * own_columns
    key_here = jnp.where(inside, key_here, -2).astype(jnp.float32)

    def process(source, target_ref, slot):
        block = source[slot]
        cell = block[4:5].astype(jnp.int32)
        start_u, start_v = cell // rows_v, cell % rows_v
        bell_u, slope_u, at_u = taps(block[2:3], start_u)
        bell_v, slope_v, at_v = taps(block[3:4], start_v)
        shape_v = (rows_v // 8, 8, width)
        hit_v = lax.broadcasted_iota(jnp.int32, shape_v, 0) == at_v[None]
        weights = jnp.concatenate([spread(bell_v, hit_v), spread(slope_v, hit_v)], axis=1)
        shape_u = (rows_u // 8, 8, width)
        hit_u = lax.broadcasted_iota(jnp.int32, shape_u, 0) == at_u[None]
        grid = tile_grid[...].reshape(2 * rows_u, rows_v)
        along = jnp.dot(
            jnp.concatenate([grid, grid], axis=1), weights, preferred_element_type=jnp.float32
        )
        residuals = []
        term_u = jnp.zeros((1, width), jnp.float32)
        term_v = jnp.zeros((1, width), jnp.float32)
        for c in range(2):
            rows = along[c * rows_u : (c + 1) * rows_u]
            with_bell = jnp.sum(jnp.where(hit_u, rows[:, :width].reshape(shape_u), 0.0), axis=0)
            with_slope = jnp.sum(jnp.where(hit_u, rows[:, width:].reshape(shape_u), 0.0), axis=0)
            model = jnp.sum(bell_u * with_bell, axis=0, keepdims=True)
            deriv_u = jnp.sum(slope_u * with_bell, axis=0, keepdims=True)
            deriv_v = jnp.sum(bell_u * with_slope, axis=0, keepdims=True)
            residual = block[c : c + 1] - model
            residuals.append(residual)
            term_u = term_u + residual * deriv_u
            term_v = term_v + residual * deriv_v
        target_ref[slot] = jnp.concatenate(residuals, axis=0)
        total_u = -2.0 * jnp.sum(term_u, axis=1, keepdims=True)
        total_v = -2.0 * jnp.sum(term_v, axis=1, keepdims=True)
        hits = (key_here == block[5:6][None]).astype(jnp.float32)
        hits = hits + (key_here == block[6:7][None]).astype(jnp.float32)
        part[...] += hits * jnp.where(first_half, total_u[None], total_v[None])

    process(stage, back, 0)

    def serve(step):
        forward(step).wait_recv()
        for j in range(size_of(step)):
            process(recv, out_blocks, first_slot(step) + j)
        backward(step).start()

    over_steps(serve)

    me = (tile * n_tm + tm) * n_pol + pol

    def hand_out(k, carry):
        where = peer(k)
        row = (where[1] * n_tm + where[2]) * n_pol + where[3]
        pltpu.make_async_remote_copy(
            src_ref=part.at[pl.ds(row, 1)],
            dst_ref=gathered.at[pl.ds(k - 1, 1)],
            send_sem=grad_send,
            recv_sem=grad_recv,
            device_id=where,
            device_id_type=MESH,
        ).start()
        return carry

    lax.fori_loop(1, count, hand_out, 0)

    res_ref[...] = jnp.zeros_like(res_ref)

    def put(slot):
        target, half, q = block_of(slot)
        filled = half < tally_ref[0, target]
        res_ref[0, 0, q] = jnp.where(filled, back[slot], 0.0)

    put(0)

    def collect(step):
        backward(step).wait_recv()
        for j in range(size_of(step)):
            put(first_slot(step) + j)

    over_steps(collect)

    everyone = pltpu.make_async_remote_copy(
        src_ref=gathered,
        dst_ref=gathered,
        send_sem=grad_send,
        recv_sem=grad_recv,
        device_id=peer(1),
        device_id_type=MESH,
    )
    everyone.wait_recv()
    total = (part[pl.ds(me, 1)][0] + jnp.sum(gathered[...], axis=0)) * scale
    grad_ref[0:1, :] = total[:, :own_columns]
    grad_ref[1:2, :] = total[:, own_columns : 2 * own_columns]
    everyone.wait_send()

    def settle(step):
        forward(step).wait_send()
        backward(step).wait_send()

    over_steps(settle)


def solution(mesh):
    sizes = tuple(mesh.shape[name] for name in AXES[1:])
    n_tile, n_tm, n_pol = sizes
    count = n_tile * n_tm * n_pol

    def local(meas, sub, cells, pairs, epochs, tallies, grid, pointing):
        blocks, width = meas.shape[2], meas.shape[4]
        holders = n_tile * n_tm
        scale = 1.0 / math.sqrt(2.0 * n_pol * holders * blocks * width / DISH_COUNT)
        own_columns = pointing.shape[1] * pointing.shape[2] // count
        slots = n_tile + 1
        vmem = pl.BlockSpec(memory_space=pltpu.VMEM)
        smem = pl.BlockSpec(memory_space=pltpu.SMEM)
        dma = pltpu.SemaphoreType.DMA
        return pl.pallas_call(
            functools.partial(kernel, sizes, scale),
            out_shape=(
                jax.ShapeDtypeStruct(meas.shape, jnp.float32),
                jax.ShapeDtypeStruct((2, own_columns), jnp.float32),
            ),
            in_specs=[vmem, vmem, vmem, smem, smem, smem, pl.BlockSpec(memory_space=pl.ANY), smem],
            out_specs=(vmem, vmem),
            scratch_shapes=[
                pltpu.VMEM((slots, 8, width), jnp.float32),
                pltpu.VMEM((slots, 8, width), jnp.float32),
                pltpu.VMEM((slots, 2, width), jnp.float32),
                pltpu.VMEM((slots, 2, width), jnp.float32),
                pltpu.VMEM((count, 1, 128), jnp.float32),
                pltpu.VMEM((count - 1, 1, 128), jnp.float32),
                pltpu.VMEM(grid.shape[2:], jnp.bfloat16),
                dma,
                dma((n_tile,)),
                dma((n_tile,)),
                dma((n_tile,)),
                dma((n_tile,)),
                dma,
                dma,
            ],
            compiler_params=pltpu.CompilerParams(
                collective_id=0, has_side_effects=True, vmem_limit_bytes=48 << 20
            ),
        )(meas, sub, cells, pairs, epochs, tallies, grid, pointing)

    return jax.shard_map(
        local,
        mesh=mesh,
        in_specs=(
            P(("group", "tile", "tm"), "pol", None, None, None),
            P(("group", "tile", "tm"), None, None, None),
            P(("group", "tile", "tm"), None, None),
            P(("group", "tile", "tm"), None, None),
            P(("group", "tile", "tm"), None),
            P(("group", "tile", "tm"), None),
            P("pol", ("group", "tile"), None, None, None),
            P(None, "group", None),
        ),
        out_specs=(
            P(("group", "tile", "tm"), "pol", None, None, None),
            P(None, ("group", "tile", "tm", "pol")),
        ),
        check_vma=False,
    )
```

time: 1160 us -> 23.5 us (0.02)
  local copies, waits for them, and re-layouts: 1020 us -> 5.23 us
  waiting for transfers between devices: 63.7 us -> 0 us
  other arithmetic: 35.5 us -> 0 us
  starting transfers between devices: 20.6 us -> 0 us
  Pallas kernels: 0 us -> 17.3 us
  between operations: 14.2 us -> 0.67 us
    gather x1 -> x0, local copies, waits for them, and re-layouts: 972 us -> none  [owner_terms(): samples = flattened_grid[:, patch_index].astype(jnp.float32)]
    unnamed x2 -> x0, waiting for transfers between devices: 53.1 us -> none
    unnamed x16 -> x17, local copies, waits for them, and re-layouts: 43.4 us -> 5.23 us
    reduce_sum x4 -> x0, other arithmetic: 31.9 us -> none  [the longest x1 30.1 us: owner_terms(): deriv_u = jnp.sum(weights_u[None] * samples, axis=1)]
    all_to_all x4 -> x0, starting transfers between devices: 20.6 us -> none  [the longest x1 6.32 us: local(): lax.all_to_all(group_whole_numbers, 'tile', split_axis=0, concat_axis=0,...]
    pallas_call x0 -> x1, Pallas kernels: none -> 17.3 us  [local(): pl.pallas_call(functools.partial(kernel, sizes, scale), out_shape=(jax.Sh...]
  transfers between devices with their start and end apart: 5 -> 0, of which waited for: 3 -> 0; matrix products, arithmetic and copies ran while one was open for 88% -> 0% of each run, Pallas kernels for 0% -> 0%
where the time goes in v1:
time: 23.5 us; the launch traced here: 23.2 us
  Pallas kernels  17.3 us (74%)
  local copies, waits for them, and re-layouts  5.23 us (22%)
  between operations  0.67 us (3%)
    pallas_call x1, Pallas kernels, local(): pl.pallas_call(functools.partial(kernel, sizes, scale), out_shape=(jax.Sh...  17.3 us
    unnamed x17, local copies, waits for them, and re-layouts  5.23 us

profile of v1, /device:TPU:0, one launch (start us, length us, event | category | flops | bytes accessed | tf_op | source)
XLA Modules:
  0.0 23.2 jit_solution(13637877062920398864)
XLA Ops:
  0.6 0.0 copy-start.6
  0.6 0.0 copy-start.5
  0.7 0.0 copy-start.3
  0.7 0.8 %copy.10.pair_ref = s32[1,8,2]{2,1,0:T(8,128)S(1)} copy(s32[1,8,2]{1,2,0:T(2,128)} %param.11) | data formatting | bytes 128 | tf_op args[3]
  1.4 0.0 copy-done.6
  1.4 0.0 copy-done.5
  1.4 0.0 copy-done.3
  1.4 0.0 copy-start
  1.4 1.2 %copy-done = bf16[1,1,2,496,512]{4,3,2,1,0:T(8,128)(2,1)S(1)} copy-done((bf16[1,1,2,496,512]{4,3,2,1,0:T(8,128)(2,1)S(1)}, bf16[1,1,2,496,512]{4,3,2,1,0:T(8,128)(2,1)}, u32[]{:S(2)}) %copy-start) | copy-done | bytes 1015832
  2.7 0.0 copy-start.1
  2.7 0.7 %copy-done.1 = f32[1,1,8,2,128]{4,3,2,1,0:T(2,128)S(1)} copy-done((f32[1,1,8,2,128]{4,3,2,1,0:T(2,128)S(1)}, f32[1,1,8,2,128]{4,3,2,1,0:T(2,128)}, u32[]{:S(2)}) %copy-start.1) | copy-done | bytes 8216
  3.4 0.0 copy-start.2
  3.4 0.7 %copy-done.2 = f32[1,8,2,128]{3,2,1,0:T(2,128)S(1)} copy-done((f32[1,8,2,128]{3,2,1,0:T(2,128)S(1)}, f32[1,8,2,128]{3,2,1,0:T(2,128)}, u32[]{:S(2)}) %copy-start.2) | copy-done | bytes 8216
  4.0 0.0 copy-start.4
  4.1 0.7 %copy-done.4 = f32[2,2,256]{2,1,0:T(2,128)S(1)} copy-done((f32[2,2,256]{2,1,0:T(2,128)S(1)}, f32[2,2,256]{2,1,0:T(2,128)}, u32[]{:S(2)}) %copy-start.4) | copy-done | bytes 4120
  4.7 17.3 %shard_map.95 = (f32[1,1,8,2,128]{4,3,2,1,0:T(2,128)S(1)}, f32[2,32]{1,0:T(2,128)S(1)}) custom-call(f32[1,1,8,2,128]{4,3,2,1,0:T(2,128)S(1)} %copy-done.1, f32[1,8,2,128]{3,2,1,0:T(2,128)S(1)} %copy-done.2, s32[1,8,128]{2,1,0:T(8,128)S(1)} %copy-done.3, s32[1,8,2]{2,1,0:T(8,128)S(1)} %copy.10.pair_ref, s32[1,8]{1,0:T(1,128)S(1)} %copy-done.5, ...), custom_call_target="tpu_custom_call" | custom-call | tf_op jit(solution)/shard_map/pallas_call | solution.py:286
  22.0 0.6 %copy.13 = f32[1,1,8,2,128]{4,3,2,1,0:T(2,128)} copy(f32[1,1,8,2,128]{4,3,2,1,0:T(2,128)S(1)} %get-tuple-element.4) | data formatting | bytes 16384
  22.6 0.6 %copy.14 = f32[2,32]{1,0:T(2,128)} copy(f32[2,32]{1,0:T(2,128)S(1)} %get-tuple-element.5) | data formatting | bytes 512
Async XLA Ops:
  0.6 0.8 %copy-start.6 = (s32[1,4]{1,0:T(1,128)S(1)}, s32[1,4]{1,0:T(1,128)}, u32[]{:S(2)}) copy-start(s32[1,4]{1,0:T(1,128)} %tally_ref.1) | copy-start | bytes 52
  0.6 0.8 %copy-start.5 = (s32[1,8]{1,0:T(1,128)S(1)}, s32[1,8]{1,0:T(1,128)}, u32[]{:S(2)}) copy-start(s32[1,8]{1,0:T(1,128)} %epoch_ref.1) | copy-start | bytes 100
  0.7 0.8 %copy-start.3 = (s32[1,8,128]{2,1,0:T(8,128)S(1)}, s32[1,8,128]{2,1,0:T(8,128)}, u32[]{:S(2)}) copy-start(s32[1,8,128]{2,1,0:T(8,128)} %cell_ref.1) | copy-start | bytes 12292
  1.4 1.2 %copy-start = (bf16[1,1,2,496,512]{4,3,2,1,0:T(8,128)(2,1)S(1)}, bf16[1,1,2,496,512]{4,3,2,1,0:T(8,128)(2,1)}, u32[]{:S(2)}) copy-start(bf16[1,1,2,496,512]{4,3,2,1,0:T(8,128)(2,1)} %grid_ref.1) | copy-start | bytes 3047428
  2.7 0.7 %copy-start.1 = (f32[1,1,8,2,128]{4,3,2,1,0:T(2,128)S(1)}, f32[1,1,8,2,128]{4,3,2,1,0:T(2,128)}, u32[]{:S(2)}) copy-start(f32[1,1,8,2,128]{4,3,2,1,0:T(2,128)} %meas_ref.1) | copy-start | bytes 24580
  3.4 0.7 %copy-start.2 = (f32[1,8,2,128]{3,2,1,0:T(2,128)S(1)}, f32[1,8,2,128]{3,2,1,0:T(2,128)}, u32[]{:S(2)}) copy-start(f32[1,8,2,128]{3,2,1,0:T(2,128)} %sub_ref.1) | copy-start | bytes 24580
  4.0 0.7 %copy-start.4 = (f32[2,2,256]{2,1,0:T(2,128)S(1)}, f32[2,2,256]{2,1,0:T(2,128)}, u32[]{:S(2)}) copy-start(f32[2,2,256]{2,1,0:T(2,128)} %point_ref.1) | copy-start | bytes 12292

commit v2 on v1

--- a/solution.py
+++ b/solution.py
@@ -37,16 +37,23 @@
 def kernel(
     sizes,
     scale,
+    meas_hbm,
+    sub_hbm,
+    cell_hbm,
+    pair_hbm,
+    epoch_hbm,
+    tally_hbm,
+    grid_ref,
+    point_hbm,
+    res_ref,
+    grad_ref,
     meas_ref,
     sub_ref,
     cell_ref,
     pair_ref,
     epoch_ref,
     tally_ref,
-    grid_ref,
     point_ref,
-    res_ref,
-    grad_ref,
     stage,
     recv,
     out_blocks,
@@ -55,6 +62,7 @@
     gathered,
     tile_grid,
     grid_sem,
+    load_sem,
     fwd_send,
     fwd_recv,
     back_send,
@@ -74,37 +82,63 @@
     own_columns = grad_ref.shape[1]
     slots = n_tile + 1
 
+    loads = [
+        pltpu.make_async_copy(source, target, load_sem.at[i])
+        for i, (source, target) in enumerate(
+            (
+                (epoch_hbm, epoch_ref),
+                (pair_hbm, pair_ref),
+                (tally_hbm, tally_ref),
+                (point_hbm, point_ref),
+                (cell_hbm, cell_ref),
+                (sub_hbm, sub_ref),
+                (meas_hbm, meas_ref),
+            )
+        )
+    ]
+    for copy in loads:
+        copy.start()
     load = pltpu.make_async_copy(grid_ref.at[0, 0], tile_grid, grid_sem)
     load.start()
+
+    def ahead(at, step, size):
+        after = at + step
+        return jnp.where(after >= size, after - size, after)
 
     def peer(k):
         return (
             group,
-            lax.rem(tile + k // (n_tm * n_pol), n_tile),
-            lax.rem(tm + (k // n_pol) % n_tm, n_tm),
-            lax.rem(pol + k % n_pol, n_pol),
-        )
+            ahead(tile, k // (n_tm * n_pol), n_tile),
+            ahead(tm, (k // n_pol) % n_tm, n_tm),
+            ahead(pol, k % n_pol, n_pol),
+        )
+
+    def over_peers(body):
+        if count <= 32:
+            for k in range(1, count):
+                body(k)
+        else:
+            lax.fori_loop(1, count, lambda k, c: (body(k), c)[1], 0)
 
     barrier = pltpu.get_barrier_semaphore()
 
-    def greet(k, carry):
+    def greet(k):
         pl.semaphore_signal(barrier, inc=1, device_id=peer(k), device_id_type=MESH)
-        return carry
-
-    lax.fori_loop(1, count, greet, 0)
+
+    over_peers(greet)
 
     def block_of(slot):
         if isinstance(slot, int):
             step, half = (slot if slot < 2 else slot - 1), int(slot == 2)
         else:
             step, half = slot - 1, 0
-        target = lax.rem(tile + step, n_tile)
+        target = ahead(tile, step, n_tile)
         return target, half, 2 * target + half
 
     def pack(slot):
         target, half, q = block_of(slot)
         time = epoch_ref[0, q]
-        first, second = pair_ref[0, q, 0], pair_ref[0, q, 1]
+        first, second = pair_ref[0, 0, q], pair_ref[0, 1, q]
         filled = half < tally_ref[0, target]
         stage[slot, 0:2, :] = meas_ref[0, 0, q]
         sub = sub_ref[0, q]
@@ -122,6 +156,8 @@
         if slots > 5:
             lax.fori_loop(5, slots, lambda s, c: (body(s), c)[1], 0)
 
+    for copy in loads:
+        copy.wait()
     over_slots(pack, 0)
     part[...] = jnp.zeros_like(part)
     pl.semaphore_wait(barrier, count - 1)
@@ -139,7 +175,7 @@
             dst_ref=recv.at[span],
             send_sem=fwd_send.at[step],
             recv_sem=fwd_recv.at[step],
-            device_id=(group, lax.rem(tile + step, n_tile), tm, pol),
+            device_id=(group, ahead(tile, step, n_tile), tm, pol),
             device_id_type=MESH,
         )
 
@@ -150,7 +186,7 @@
             dst_ref=back.at[span],
             send_sem=back_send.at[step],
             recv_sem=back_recv.at[step],
-            device_id=(group, lax.rem(tile - step + n_tile, n_tile), tm, pol),
+            device_id=(group, ahead(tile, n_tile - step, n_tile), tm, pol),
             device_id_type=MESH,
         )
 
@@ -217,7 +253,7 @@
 
     me = (tile * n_tm + tm) * n_pol + pol
 
-    def hand_out(k, carry):
+    def hand_out(k):
         where = peer(k)
         row = (where[1] * n_tm + where[2]) * n_pol + where[3]
         pltpu.make_async_remote_copy(
@@ -228,9 +264,8 @@
             device_id=where,
             device_id_type=MESH,
         ).start()
-        return carry
-
-    lax.fori_loop(1, count, hand_out, 0)
+
+    over_peers(hand_out)
 
     res_ref[...] = jnp.zeros_like(res_ref)
 
@@ -281,7 +316,8 @@
         own_columns = pointing.shape[1] * pointing.shape[2] // count
         slots = n_tile + 1
         vmem = pl.BlockSpec(memory_space=pltpu.VMEM)
-        smem = pl.BlockSpec(memory_space=pltpu.SMEM)
+        hbm = pl.BlockSpec(memory_space=pltpu.HBM)
+        pairs = jnp.swapaxes(pairs, 1, 2)
         dma = pltpu.SemaphoreType.DMA
         return pl.pallas_call(
             functools.partial(kernel, sizes, scale),
@@ -289,9 +325,16 @@
                 jax.ShapeDtypeStruct(meas.shape, jnp.float32),
                 jax.ShapeDtypeStruct((2, own_columns), jnp.float32),
             ),
-            in_specs=[vmem, vmem, vmem, smem, smem, smem, pl.BlockSpec(memory_space=pl.ANY), smem],
+            in_specs=[hbm] * 8,
             out_specs=(vmem, vmem),
             scratch_shapes=[
+                pltpu.VMEM(meas.shape, jnp.float32),
+                pltpu.VMEM(sub.shape, jnp.float32),
+                pltpu.VMEM(cells.shape, jnp.int32),
+                pltpu.SMEM(pairs.shape, jnp.int32),
+                pltpu.SMEM(epochs.shape, jnp.int32),
+                pltpu.SMEM(tallies.shape, jnp.int32),
+                pltpu.SMEM(pointing.shape, jnp.float32),
                 pltpu.VMEM((slots, 8, width), jnp.float32),
                 pltpu.VMEM((slots, 8, width), jnp.float32),
                 pltpu.VMEM((slots, 2, width), jnp.float32),
@@ -300,6 +343,7 @@
                 pltpu.VMEM((count - 1, 1, 128), jnp.float32),
                 pltpu.VMEM(grid.shape[2:], jnp.bfloat16),
                 dma,
+                dma((7,)),
                 dma((n_tile,)),
                 dma((n_tile,)),
                 dma((n_tile,)),
@@ -308,7 +352,7 @@
                 dma,
             ],
             compiler_params=pltpu.CompilerParams(
-                collective_id=0, has_side_effects=True, vmem_limit_bytes=48 << 20
+                collective_id=0, has_side_effects=True, vmem_limit_bytes=60 << 20
             ),
         )(meas, sub, cells, pairs, epochs, tallies, grid, pointing)
 

time: 23.5 us -> 19.4 us (0.83)
  local copies, waits for them, and re-layouts: 5.23 us -> 1.86 us
  Pallas kernels: 17.3 us -> 16.7 us
    unnamed x17 -> x4, local copies, waits for them, and re-layouts: 5.23 us -> 1.86 us
    pallas_call x1, Pallas kernels: 17.3 us -> 16.7 us  [local(): pl.pallas_call(functools.partial(kernel, sizes, scale), out_shape=(jax.Sh...]
where the time goes in v2:
time: 19.4 us; the launch traced here: 19.2 us
  Pallas kernels  16.7 us (86%)
  local copies, waits for them, and re-layouts  1.86 us (10%)
  between operations  0.65 us (3%)
    pallas_call x1, Pallas kernels, local(): pl.pallas_call(functools.partial(kernel, sizes, scale), out_shape=(jax.Sh...  16.7 us
    unnamed x4, local copies, waits for them, and re-layouts  1.86 us

profile of v2, /device:TPU:0, one launch (start us, length us, event | category | flops | bytes accessed | tf_op | source)
XLA Modules:
  0.0 19.2 jit_solution(7777276376283640560)
XLA Ops:
  0.6 16.7 %shard_map.95 = (f32[1,1,8,2,128]{4,3,2,1,0:T(2,128)}, f32[2,32]{1,0:T(2,128)}) custom-call(f32[1,1,8,2,128]{4,3,2,1,0:T(2,128)} %meas_hbm.1, f32[1,8,2,128]{3,2,1,0:T(2,128)} %sub_hbm.1, s32[1,8,128]{2,1,0:T(8,128)} %cell_hbm.1, s32[1,2,8]{2,1,0:T(2,128)} %bitcast.1, s32[1,8]{1,0:T(1,128)} %epoch_hbm.1, s32[1,4]{1,0:T(1,128)} %tally_hbm.1, ...), custom_call_target="tpu_custom_call" | custom-call | tf_op jit(solution)/shard_map/pallas_call | solution.py:322
  17.3 0.0 copy-start
  17.3 1.3 %copy.12 = f32[1,1,8,2,128]{4,3,2,1,0:T(2,128)} copy(f32[1,1,8,2,128]{4,3,2,1,0:T(2,128)} %get-tuple-element.4) | data formatting | bytes 16384
  18.6 0.0 copy-done
  18.6 0.6 %copy.13 = f32[2,32]{1,0:T(2,128)} copy(f32[2,32]{1,0:T(2,128)S(1)} %copy-done) | data formatting | bytes 512
Async XLA Ops:
  17.3 1.3 %copy-start = (f32[2,32]{1,0:T(2,128)S(1)}, f32[2,32]{1,0:T(2,128)}, u32[]{:S(2)}) copy-start(f32[2,32]{1,0:T(2,128)} %get-tuple-element.5) | copy-start | bytes 772
